TPU v7x, 128 devices: a whole 4x4x4 slice. The times are simulated.
128 devices in a mesh: req: 32 (over y, z, core), grp: 4 (over x).
Axes of the slice: x: 4, y: 4, z: 4, core: 2. Of those that a mesh axis runs over, the one named last changes fastest.
Arguments:
- residual_in: bfloat16 [2048, 2048], P('grp'), may hold values from -6 to 6
- mixer_in: bfloat16 [2048, 3, 2048], P('grp', None, 'req'), may hold values from -6 to 6
- forget_floor: float32 [2048], replicated, may hold values from 0.3 to 0.97
- conv_weight: float32 [4, 2048], P(None, 'req'), may hold values from -3 to 3
- conv_edges: bfloat16 [128, 3, 2048], P('grp', None, 'req'), may hold values from -6 to 6
- state_in: float32 [128, 2048, 128], P('grp', 'req'), may hold values from -6 to 6
- accepted: int32 [128], P('grp'), may hold values from 0 to 16
- home_slot: int32 [128], replicated, may hold values from 0 to 127, each once
- gain_mixer: float32 [2048], P('req'), may hold values from 0.1 to 1.9
- w_out: bfloat16 [2048, 2048], P('req'), may hold values from -0.25 to 0.25
- gain_mlp: float32 [2048], replicated, may hold values from 0.1 to 1.9
- w_gate: bfloat16 [2048, 5632], P(None, 'req'), may hold values from -0.125 to 0.125
- w_up: bfloat16 [2048, 5632], P(None, 'req'), may hold values from -0.125 to 0.125
- w_down: bfloat16 [5632, 2048], P('req'), may hold values from -0.15625 to 0.15625
- gain_next: float32 [2048], replicated, may hold values from 0.1 to 1.9
- w_next: bfloat16 [2048, 3, 2048], P(None, None, 'req'), may hold values from -0.125 to 0.125
Outputs:
- next_mixer: bfloat16 [2048, 3, 2048], P('grp', None, 'req')
- kept_state: float32 [128, 2048, 128], P('grp', 'req')
- kept_edges: bfloat16 [128, 3, 2048], P('grp', None, 'req')
Inputs may be any that keep to these rules, and one draw needn't show every extreme that they name: `home_slot`: every row of the kept outputs is the home of exactly one request.
All inputs are finite; a program needn't handle non-finite values.
Results may differ from a plain program's by a relative error of at most 0.029.
Values may be sent and summed in bfloat16 or wider, within the bound.
A program may use at most 64 MiB of HBM per device.

v0:
```python
import jax
import jax.numpy as jnp
from jax import lax
from jax.sharding import PartitionSpec as P

EPSILON = 1e-06


def partner_2(block, axis, apart):
    count = lax.axis_size(axis)
    route = []
    for low in range(count):
        high = low | 1 << apart
        if high != low and high < count:
            route += [(low, high), (high, low)]
    return lax.ppermute(block, axis, route)


def scaled_norm(values_in, gain_row):
    widened = values_in.astype(jnp.float32)
    factor = lax.rsqrt(jnp.mean(widened * widened, axis=1, keepdims=True) + EPSILON)
    return (widened * factor * gain_row).astype(jnp.bfloat16)


def per_device(
    residual_in,
    mixer_in,
    forget_floor,
    conv_weight,
    conv_edges,
    state_in,
    accepted,
    home_slot,
    gain_mixer,
    w_out,
    gain_mlp,
    w_gate,
    w_up,
    w_down,
    gain_next,
    w_next,
):
    token_rows = residual_in.shape[0]
    model_width = residual_in.shape[1]
    local_width = mixer_in.shape[2]
    requests = state_in.shape[0]
    key_width = state_in.shape[2]
    draft_steps = token_rows // requests
    tap_count = conv_weight.shape[0]
    member = lax.axis_index("req")
    own_halves = mixer_in[:, 0:2]
    partner = partner_2(own_halves, "req", 0)
    lower_half = member % 2 == 0
    key_side = jnp.where(
        lower_half,
        jnp.concatenate([own_halves, partner], axis=2),
        jnp.concatenate([partner, own_halves], axis=2),
    )
    head_count = local_width // local_width
    key_start = member * local_width // key_width * key_width
    forget_low = lax.dynamic_slice_in_dim(forget_floor, key_start, head_count * key_width, 0)
    query = jax.nn.silu(key_side[:, 0].astype(jnp.float32))
    forget = forget_low + (1.0 - forget_low) * jax.nn.sigmoid(key_side[:, 1].astype(jnp.float32))
    keyed = 1.0 - forget
    sequence = jnp.concatenate(
        [conv_edges, mixer_in[:, 2].reshape(requests, draft_steps, local_width)], axis=1
    )
    seq_float = sequence.astype(jnp.float32)
    conv_input = sum(
        (
            conv_weight[offset] * seq_float[:, offset : offset + draft_steps]
            for offset in range(tap_count)
        )
    )

    def by_step(array_in, inner_width):
        shaped = array_in.reshape(requests, draft_steps, head_count, inner_width)
        return jnp.moveaxis(shaped, 1, 0)

    step_inputs = (
        by_step(query, key_width),
        by_step(forget, key_width),
        by_step(keyed, key_width),
        by_step(conv_input, local_width),
    )
    head_scale = key_width ** (-0.5)

    def advance(carry, inputs_now):
        current, kept, counter = carry
        q_step, f_step, k_step, v_step = inputs_now
        current = f_step[:, :, None, :] * current + v_step[:, :, :, None] * k_step[:, :, None, :]
        output = jnp.sum(current * q_step[:, :, None, :], axis=3) * head_scale
        kept = jnp.where((counter + 1 == accepted)[:, None, None, None], current, kept)
        return ((current, kept, counter + 1), output)

    begin_state = state_in.reshape(requests, head_count, local_width, key_width)
    carry_out, outputs = lax.scan(advance, (begin_state, begin_state, jnp.int32(0)), step_inputs)
    kept_local = carry_out[1].reshape(requests, local_width, key_width)
    mixed = jnp.moveaxis(outputs, 0, 1).reshape(token_rows, local_width)
    gained = (mixed * gain_mixer).astype(jnp.bfloat16)
    partial_squares = jnp.sum(mixed * mixed, axis=1)
    mixer_terms = jnp.dot(gained, w_out, preferred_element_type=jnp.float32)
    mixer_sum, squares = (
        lax.psum(mixer_terms.astype(jnp.bfloat16), "req").astype(jnp.float32),
        lax.psum(partial_squares.astype(jnp.bfloat16), "req").astype(jnp.float32),
    )
    attn = mixer_sum * lax.rsqrt(squares[:, None] / model_width + EPSILON)
    first = (residual_in.astype(jnp.float32) + attn).astype(jnp.bfloat16)
    normed = scaled_norm(first, gain_mlp)
    gate = jnp.dot(normed, w_gate, preferred_element_type=jnp.float32)
    up_part = jnp.dot(normed, w_up, preferred_element_type=jnp.float32)
    hidden = (jax.nn.silu(gate) * up_part).astype(jnp.bfloat16)
    next_weight = w_next.reshape(model_width, 3 * local_width)
    down_terms = jnp.dot(hidden, w_down, preferred_element_type=jnp.float32)
    down = lax.psum(down_terms.astype(jnp.bfloat16), "req").astype(jnp.float32)
    second = (first.astype(jnp.float32) + down).astype(jnp.bfloat16)
    final_norm = scaled_norm(second, gain_next)
    next_flat = jnp.dot(final_norm, next_weight, preferred_element_type=jnp.float32)
    next_mixer = next_flat.astype(jnp.bfloat16).reshape(token_rows, 3, local_width)
    edge_count = conv_edges.shape[1]
    edge_index = accepted[:, None] + jnp.arange(edge_count, dtype=jnp.int32)[None, :]
    kept_edge = jnp.take_along_axis(sequence, edge_index[:, :, None], axis=1)
    group_start = lax.axis_index("grp") * requests
    empty_state = jnp.zeros_like(kept_local)
    empty_edges = jnp.zeros(kept_edge.shape, jnp.float32)
    state_acc = empty_state
    edge_acc = empty_edges
    state_piece = lax.all_gather(kept_local.astype(jnp.bfloat16), "grp", axis=0, tiled=True).astype(
        jnp.float32
    )
    edge_piece = lax.all_gather(
        kept_edge.astype(jnp.float32).astype(jnp.bfloat16), "grp", axis=0, tiled=True
    ).astype(jnp.float32)
    target = home_slot - group_start
    inside = (target >= 0) & (target < requests)
    target = jnp.where(inside, target, requests)
    state_acc = state_acc.at[target].set(state_piece, mode="drop")
    edge_acc = edge_acc.at[target].set(edge_piece, mode="drop")
    return (next_mixer, state_acc, edge_acc.astype(jnp.bfloat16))


def solution(mesh):
    in_specs = (
        P("grp", None),
        P("grp", None, "req"),
        P(),
        P(None, "req"),
        P("grp", None, "req"),
        P("grp", "req", None),
        P("grp"),
        P(),
        P("req"),
        P("req", None),
        P(),
        P(None, "req"),
        P(None, "req"),
        P("req", None),
        P(),
        P(None, None, "req"),
    )
    out_specs = (P("grp", None, "req"), P("grp", "req", None), P("grp", None, "req"))
    return jax.shard_map(
        per_device, mesh=mesh, in_specs=in_specs, out_specs=out_specs, check_vma=False
    )
```

profile of v0, /device:TPU:1, one launch (start us, length us, event | category | flops | bytes accessed | tf_op | source)
XLA Modules:
  0.0 312.3 jit_solution(15410177543315030601)
XLA Ops:
  8.1 1.3 copy.83
  9.3 0.9 slice.36
  10.5 1.5 collective-permute-start
  17.4 35.0 %while.17 = (s32[]{:T(128)}, f32[32,1,64,128]{3,2,1,0:T(8,128)S(1)}, bf16[32,1,64,128]{3,2,1,0:T(8,128)(2,1)S(1)}, f32[16,32,1,64]{3,2,1,0:T(1,128)S(1)}, f32[16...) while((s32[]{:T(128)}, ...), condition=%wide.region_2.3_spmd, body=%wide.region_0.2_spmd.sunk | while | flops 1572898 | bytes 4424001 | solution.py:97
  17.4 0.9 constant_dynamic-slice_fusion.5
  18.4 0.9 multiply_reduce_fusion.3
  19.6 0.9 constant_dynamic-slice_fusion.5
  20.6 0.9 multiply_reduce_fusion.3
  21.8 0.9 constant_dynamic-slice_fusion.5
  22.8 0.9 multiply_reduce_fusion.3
  24.0 0.9 constant_dynamic-slice_fusion.5
  25.0 0.9 multiply_reduce_fusion.3
  26.2 0.9 constant_dynamic-slice_fusion.5
  27.2 0.9 multiply_reduce_fusion.3
  28.4 0.9 constant_dynamic-slice_fusion.5
  29.4 0.9 multiply_reduce_fusion.3
  30.6 0.9 constant_dynamic-slice_fusion.5
  31.5 0.9 multiply_reduce_fusion.3
  32.7 0.9 constant_dynamic-slice_fusion.5
  33.7 0.9 multiply_reduce_fusion.3
  34.9 0.9 constant_dynamic-slice_fusion.5
  35.9 0.9 multiply_reduce_fusion.3
  37.1 0.9 constant_dynamic-slice_fusion.5
  39.3 0.9 constant_dynamic-slice_fusion.5
  40.3 0.9 multiply_reduce_fusion.3
  41.5 0.9 constant_dynamic-slice_fusion.5
  43.7 0.9 constant_dynamic-slice_fusion.5
  44.7 0.9 multiply_reduce_fusion.3
  45.9 0.9 constant_dynamic-slice_fusion.5
  48.0 0.9 constant_dynamic-slice_fusion.5
  49.0 0.9 multiply_reduce_fusion.3
  50.2 0.9 constant_dynamic-slice_fusion.5
  52.6 2.9 convolution_convert_fusion.1
  55.6 1.1 multiply_reduce_fusion.1
  57.0 63.9 %psum.22 = bf16[512]{0:T(512)(128)(2,1)S(1)} all-reduce(bf16[512]{0:T(512)(128)(2,1)S(1)} %convert_element_type.109), channel_id=1, replica_groups=mesh['req'=32,'grp'=4] {'req'}, use_global_device_ids=true, to_apply=%region_5.6 | all-reduce | flops 512 | bytes 2048 | tf_op jit(solution)/shard_map/psum | solution.py:105
  120.9 44.4 %all-reduce.3.cloned.1.call-done = bf16[512,2048]{1,0:T(8,128)(2,1)} async-done(((bf16[512,2048]{1,0:T(8,128)(2,1)}), bf16[512,2048]{1,0:T(8,128)(2,1)}) %all-reduce.3.cloned.1.call-update) | async-done | bytes 2097168 | tf_op jit(solution)/shard_map/psum | solution.py:104
  165.3 3.2 %fusion.3 = (f32[512]{0:T(512)S(1)}, bf16[512,2048]{1,0:T(8,128)(2,1)S(1)}) fusion(f32[512]{0:T(512)S(1)} %add_rsqrt_fusion.2, bf16[512,2048]{1,0:T(8,128)(2,1)} %all-reduce.3.cloned.1.call-done, bf16[512,2048]{1,0:T(8,128)(2,1)} %param.18), kind=kLoop, calls=%fused_computation.21 | loop fusion | flops 8388096 | bytes 6295552 | tf_op jit(solution)/shard_map/reduce_sum | solution.py:21
  168.5 2.0 fusion.18
  170.6 4.3 %convolution_convert_fusion = bf16[512,2048]{1,0:T(8,128)(2,1)} fusion(bf16[176,2048]{1,0:T(8,128)(2,1)} %param.31, bf16[2048,176]{0,1:T(8,128)(2,1)} %param.30, bf16[512,2048]{1,0:T(8,128)(2,1)S(1)} %get-tuple-element.226, f32[2048]{0:T(1024)S(1)} %copy-done.8, f32[512]{0:T(512)S(1)} %add_rsqrt_fusion.1, f32[512,176]{0,1:T(8,128)S(1)} %fusion.18), kind=kOutput, calls=%fused_computation.26 | convolution fusion | flops 743981056 | bytes 6006784 | tf_op jit(solution)/shard_map/dot_general | solution.py:114
  175.6 1.5 gather_fusion
  177.4 9.7 %all_gather.7 = bf16[128,3,64]{2,0,1:T(8,128)(2,1)S(1)} all-gather(bf16[32,3,64]{2,0,1:T(8,128)(2,1)S(1)} %copy.53), channel_id=1, replica_groups=mesh['req'=32,'grp'=4] {'grp'}, dimensions={0}, use_global_device_ids=true | all-gather | bytes 61440 | tf_op jit(solution)/shard_map/all_gather | solution.py:131
  187.4 4.6 %scatter_fusion.1 = f32[32,3,64]{2,1,0:T(4,128)S(1)} fusion(f32[32,3,64]{2,1,0:T(4,128)S(1)} %broadcast_in_dim.72, s32[128]{0:T(128)S(1)} %compare_select_fusion.2, f32[128,3,64]{2,1,0:T(4,128)S(1)} %copy.55), kind=kCustom, calls=%fused_computation.2 | custom fusion | bytes 295424 | tf_op jit(solution)/shard_map/scatter | solution.py:138
  192.7 90.1 %all-reduce.5.cloned.1.call-done = bf16[512,2048]{1,0:T(8,128)(2,1)} async-done(((bf16[512,2048]{1,0:T(8,128)(2,1)}), bf16[512,2048]{1,0:T(8,128)(2,1)}) %all-reduce.5.cloned.1.call-update) | async-done | bytes 2097168 | tf_op jit(solution)/shard_map/psum | solution.py:115
  282.7 2.5 fusion
  285.3 1.8 fusion.11
  287.0 4.0 %bitcast_convert_fusion = f32[128,64,128]{2,1,0:T(8,128)} fusion(bf16[128,1,64,128]{3,2,1,0:T(8,128)(2,1)} %all-gather.3.cloned.1.call-done), kind=kLoop, calls=%fused_computation.29 | loop fusion | flops 1048576 | bytes 6291456 | tf_op jit(solution)/shard_map/convert_element_type | solution.py:128
  291.1 12.8 %scatter_fusion = f32[32,64,128]{2,1,0:T(8,128)S(1)} fusion(f32[32,64,128]{2,1,0:T(8,128)S(1)} %broadcast_in_dim.70, s32[128]{0:T(128)S(1)} %compare_select_fusion.2, f32[128,64,128]{2,1,0:T(8,128)} %bitcast_convert_fusion), kind=kCustom, calls=%fused_computation.1 | custom fusion | bytes 12583424 | tf_op jit(solution)/shard_map/scatter | solution.py:137
  303.9 1.0 copy-done.1
  (165 shorter events, 16.1 us)
Async XLA Ops:
  8.0 277.2 %copy-start = (bf16[2048,3,64]{0,2,1:T(8,128)(2,1)S(1)}, bf16[2048,3,64]{0,2,1:T(8,128)(2,1)}, u32[]{:S(2)}) copy-start(bf16[2048,3,64]{0,2,1:T(8,128)(2,1)} %param.33) | copy-start | bytes 2359300
  8.0 157.3 %all-reduce.3.cloned.1.call-start = ((), (), s32[]{:S(2)}) async-start(), calls=%async_computation | async-start | bytes 4194304 | tf_op jit(solution)/shard_map/psum | solution.py:104
  9.3 8.1 %copy-start.7 = (s32[32]{0:T(128)S(1)}, s32[32]{0:T(128)}, u32[]{:S(2)}) copy-start(s32[32]{0:T(128)} %param.24) | copy-start | bytes 388
  10.5 5.8 %collective-permute-start = (bf16[512,2,64]{2,0,1:T(8,128)(2,1)S(1)}, bf16[512,2,64]{2,0,1:T(8,128)(2,1)S(1)}, u32[]{:S(2)}, u32[]{:S(2)}) collective-permute-start(bf16[512,2,64]{2,0,1:T(8,128)(2,1)S(1)} %copy.60), channel_id=1, source_target_pairs={{0,4},{4,0},{8,12},{12,8},{16,20},{20,16},{24,28},{28,24},{32,36},... | collective-permute-start | bytes 393224 | tf_op jit(solution)/shard_map/ppermute | solution.py:16
  14.5 0.7 copy-start.4
  17.4 35.1 %copy-start.6 = (f32[64]{0:T(128)S(1)}, f32[64]{0:T(128)}, u32[]{:S(2)}) copy-start(f32[64]{0:T(128)} %param.26) | copy-start | bytes 772
  52.4 116.1 %copy-start.2 = (bf16[32,1,64,128]{3,2,1,0:T(8,128)(2,1)}, bf16[32,1,64,128]{3,2,1,0:T(8,128)(2,1)S(1)}, u32[]{:S(2)}) copy-start(bf16[32,1,64,128]{3,2,1,0:T(8,128)(2,1)S(1)} %get-tuple-element.159) | copy-start | bytes 1572868
  55.6 113.0 %copy-start.8 = (f32[2048]{0:T(1024)S(1)}, f32[2048]{0:T(1024)}, u32[]{:S(2)}) copy-start(f32[2048]{0:T(1024)} %param.28) | copy-start | bytes 24580
  55.6 227.1 %all-reduce.5.cloned.1.call-start = ((), (), s32[]{:S(2)}) async-start(), calls=%async_computation.1 | async-start | bytes 4194304 | tf_op jit(solution)/shard_map/psum | solution.py:115
  170.6 5.1 %copy-start.5 = (bf16[32,19,64]{2,0,1:T(8,128)(2,1)S(1)}, bf16[32,19,64]{2,0,1:T(8,128)(2,1)}, u32[]{:S(2)}) copy-start(bf16[32,19,64]{2,0,1:T(8,128)(2,1)} %copy-done.4) | copy-start | bytes 233476
  170.6 16.8 %copy-start.10 = (s32[128]{0:T(128)S(1)}, s32[128]{0:T(128)}, u32[]{:S(2)}) copy-start(s32[128]{0:T(128)} %param.25) | copy-start | bytes 1540
  174.8 110.4 %copy-start.9 = (f32[2048]{0:T(1024)S(1)}, f32[2048]{0:T(1024)}, u32[]{:S(2)}) copy-start(f32[2048]{0:T(1024)} %param.32) | copy-start | bytes 24580
  174.9 112.2 %all-gather.3.cloned.1.call-start = ((), (), s32[]{:S(2)}) async-start(), calls=%async_computation.2 | async-start | bytes 2621440 | tf_op jit(solution)/shard_map/all_gather | solution.py:128
  282.7 2.5 copy-start.3
  303.9 1.0 copy-start.1
Sparse Core Ops, SparseCore 0:
  55.7 109.5 all-reduce.2
  175.0 107.6 all-reduce.4
Sparse Core Ops, SparseCore 1:
  177.6 30.1 all-gather.2
where the time goes:
time: 313 us; the launch traced here: 312 us
  waiting for transfers between devices  135 us (43%)
  blocking collectives  73.7 us (24%)
  local copies, waits for them, and re-layouts  42.7 us (14%)
  other arithmetic  31.4 us (10%)
  between operations  15.9 us (5%)
  matrix products  11 us (4%)
    psum x1, waiting for transfers between devices, per_device(): down = lax.psum(down_terms.astype(jnp.bfloat16), 'req').astype(jnp.float32)  90.1 us
    psum x1, blocking collectives, per_device(): lax.psum(partial_squares.astype(jnp.bfloat16), 'req').astype(jnp.float32)  63.9 us
    psum x1, waiting for transfers between devices, per_device(): lax.psum(mixer_terms.astype(jnp.bfloat16), 'req').astype(jnp.float32)  44.4 us
    dynamic_slice x32, local copies, waits for them, and re-layouts, per_device(): lax.scan(advance, (begin_state, begin_state, jnp.int32(0)), step_inputs)  15.3 us
    reduce_sum x16, other arithmetic, advance(): output = jnp.sum(current * q_step[:, :, None, :], axis=3) * head_scale  14.5 us
    scatter x1, local copies, waits for them, and re-layouts, per_device(): state_acc = state_acc.at[target].set(state_piece, mode='drop')  12.8 us
    all_gather x1, blocking collectives, per_device(): lax.all_gather(kept_edge.astype(jnp.float32).astype(jnp.bfloat16), 'grp',...  9.73 us
  transfers between devices with their start and end apart: 4, of which 2 were waited for; matrix products, arithmetic and copies ran while one was open for 5% of the time, Pallas kernels for 0%

commit v1 on v0

--- a/solution.py
+++ b/solution.py
@@ -128,8 +128,14 @@
     state_piece = lax.all_gather(kept_local.astype(jnp.bfloat16), "grp", axis=0, tiled=True).astype(
         jnp.float32
     )
-    edge_piece = lax.all_gather(
-        kept_edge.astype(jnp.float32).astype(jnp.bfloat16), "grp", axis=0, tiled=True
+    edge_piece = jnp.concatenate(
+        lax.all_to_all(
+            jnp.stack([kept_edge.astype(jnp.float32).astype(jnp.bfloat16)] * lax.axis_size("grp")),
+            "grp",
+            0,
+            0,
+        ),
+        axis=0,
     ).astype(jnp.float32)
     target = home_slot - group_start
     inside = (target >= 0) & (target < requests)

time: 313 us -> 314 us (level)
  blocking collectives: 73.7 us -> 63.9 us
  waiting for transfers between devices: 135 us -> 140 us
  starting transfers between devices: 1.62 us -> 5.59 us
    all_gather x1 -> x0, blocking collectives: 9.73 us -> none  [per_device(): lax.all_gather(kept_edge.astype(jnp.float32).astype(jnp.bfloat16), 'grp',...]
    all_to_all x0 -> x1, waiting for transfers between devices: none -> 4.38 us  [per_device(): lax.all_to_all(jnp.stack([kept_edge.astype(jnp.float32).astype(jnp.bfloat...]
    all_to_all x0 -> x1, starting transfers between devices: none -> 3.97 us  [per_device(): lax.all_to_all(jnp.stack([kept_edge.astype(jnp.float32).astype(jnp.bfloat...]
  transfers between devices with their start and end apart: 4 -> 5, of which waited for: 2 -> 3; matrix products, arithmetic and copies ran while one was open for 5% -> 6% of each run, Pallas kernels for 0% -> 0%
where the time goes in v1:
time: 314 us; the launch traced here: 312 us
  waiting for transfers between devices  140 us (45%)
  blocking collectives  63.9 us (20%)
  local copies, waits for them, and re-layouts  43.5 us (14%)
  other arithmetic  31.4 us (10%)
  between operations  15.9 us (5%)
  matrix products  11 us (4%)
  starting transfers between devices  5.59 us (2%)
    psum x1, waiting for transfers between devices, per_device(): down = lax.psum(down_terms.astype(jnp.bfloat16), 'req').astype(jnp.float32)  90.7 us
    psum x1, blocking collectives, per_device(): lax.psum(partial_squares.astype(jnp.bfloat16), 'req').astype(jnp.float32)  63.9 us
    psum x1, waiting for transfers between devices, per_device(): lax.psum(mixer_terms.astype(jnp.bfloat16), 'req').astype(jnp.float32)  44.4 us
    dynamic_slice x32, local copies, waits for them, and re-layouts, per_device(): lax.scan(advance, (begin_state, begin_state, jnp.int32(0)), step_inputs)  15.3 us
    reduce_sum x16, other arithmetic, advance(): output = jnp.sum(current * q_step[:, :, None, :], axis=3) * head_scale  14.5 us
    scatter x1, local copies, waits for them, and re-layouts, per_device(): state_acc = state_acc.at[target].set(state_piece, mode='drop')  12.8 us
  transfers between devices with their start and end apart: 5, of which 3 were waited for; matrix products, arithmetic and copies ran while one was open for 6% of the time, Pallas kernels for 0%

profile of v1, /device:TPU:1, one launch (start us, length us, event | category | flops | bytes accessed | tf_op | source)
XLA Modules:
  0.0 312.4 jit_solution(725874935502439801)
XLA Ops:
  8.1 1.3 copy.95
  9.3 0.9 slice.36
  10.5 1.5 collective-permute-start
  17.4 35.0 %while.17 = (s32[]{:T(128)}, f32[32,1,64,128]{3,2,1,0:T(8,128)S(1)}, bf16[32,1,64,128]{3,2,1,0:T(8,128)(2,1)S(1)}, f32[16,32,1,64]{3,2,1,0:T(1,128)S(1)}, f32[16...) while((s32[]{:T(128)}, ...), condition=%wide.region_2.3_spmd, body=%wide.region_0.2_spmd.sunk | while | flops 1572898 | bytes 4424001 | solution.py:97
  17.4 0.9 constant_dynamic-slice_fusion.5
  18.4 0.9 multiply_reduce_fusion.3
  19.6 0.9 constant_dynamic-slice_fusion.5
  20.6 0.9 multiply_reduce_fusion.3
  21.8 0.9 constant_dynamic-slice_fusion.5
  22.8 0.9 multiply_reduce_fusion.3
  24.0 0.9 constant_dynamic-slice_fusion.5
  25.0 0.9 multiply_reduce_fusion.3
  26.2 0.9 constant_dynamic-slice_fusion.5
  27.2 0.9 multiply_reduce_fusion.3
  28.4 0.9 constant_dynamic-slice_fusion.5
  29.4 0.9 multiply_reduce_fusion.3
  30.6 0.9 constant_dynamic-slice_fusion.5
  31.5 0.9 multiply_reduce_fusion.3
  32.7 0.9 constant_dynamic-slice_fusion.5
  34.9 0.9 constant_dynamic-slice_fusion.5
  35.9 0.9 multiply_reduce_fusion.3
  37.1 0.9 constant_dynamic-slice_fusion.5
  39.3 0.9 constant_dynamic-slice_fusion.5
  40.3 0.9 multiply_reduce_fusion.3
  41.5 0.9 constant_dynamic-slice_fusion.5
  43.7 0.9 constant_dynamic-slice_fusion.5
  44.7 0.9 multiply_reduce_fusion.3
  45.9 0.9 constant_dynamic-slice_fusion.5
  48.0 0.9 constant_dynamic-slice_fusion.5
  49.0 0.9 multiply_reduce_fusion.3
  50.2 0.9 constant_dynamic-slice_fusion.5
  52.6 2.9 convolution_convert_fusion.1
  55.6 1.1 multiply_reduce_fusion.1
  56.9 63.9 %psum.22 = bf16[512]{0:T(512)(128)(2,1)S(1)} all-reduce(bf16[512]{0:T(512)(128)(2,1)S(1)} %convert_element_type.112), channel_id=1, replica_groups=mesh['req'=32,'grp'=4] {'req'}, use_global_device_ids=true, to_apply=%region_5.6 | all-reduce | flops 512 | bytes 2048 | tf_op jit(solution)/shard_map/psum | solution.py:105
  120.9 44.4 %all-reduce.3.cloned.1.call-done = bf16[512,2048]{1,0:T(8,128)(2,1)} async-done(((bf16[512,2048]{1,0:T(8,128)(2,1)}), bf16[512,2048]{1,0:T(8,128)(2,1)}) %all-reduce.3.cloned.1.call-update) | async-done | bytes 2097168 | tf_op jit(solution)/shard_map/psum | solution.py:104
  165.3 3.2 %fusion.3 = (f32[512]{0:T(512)S(1)}, bf16[512,2048]{1,0:T(8,128)(2,1)S(1)}) fusion(f32[512]{0:T(512)S(1)} %add_rsqrt_fusion.2, bf16[512,2048]{1,0:T(8,128)(2,1)} %all-reduce.3.cloned.1.call-done, bf16[512,2048]{1,0:T(8,128)(2,1)} %param.18), kind=kLoop, calls=%fused_computation.21 | loop fusion | flops 8388096 | bytes 6295552 | tf_op jit(solution)/shard_map/reduce_sum | solution.py:21
  168.5 2.0 fusion.18
  170.6 4.2 %convolution_convert_fusion = bf16[512,2048]{1,0:T(8,128)(2,1)} fusion(bf16[176,2048]{1,0:T(8,128)(2,1)} %param.31, bf16[2048,176]{0,1:T(8,128)(2,1)} %param.30, bf16[512,2048]{1,0:T(8,128)(2,1)S(1)} %get-tuple-element.238, f32[2048]{0:T(1024)S(1)} %copy-done.8, f32[512]{0:T(512)S(1)} %add_rsqrt_fusion.1, f32[512,176]{0,1:T(8,128)S(1)} %fusion.18), kind=kOutput, calls=%fused_computation.26 | convolution fusion | flops 743981056 | bytes 6006784 | tf_op jit(solution)/shard_map/dot_general | solution.py:114
  175.6 1.5 gather_fusion
  178.2 4.0 %all-to-all-start = ((bf16[4,2,3072]{2,1,0:T(2,128)(2,1)}), bf16[4,2,3072]{2,1,0:T(2,128)(2,1)S(1)}, u32[]{:S(2)}, u32[]{:S(2)}) async-start(bf16[4,2,3072]{2,1,0:T(2,128)(2,1)} %reshape.293), calls=%async_computation | async-start | bytes 98304 | tf_op jit(solution)/shard_map/all_to_all | solution.py:132
  182.1 4.4 %all-to-all-done = bf16[4,2,3072]{2,1,0:T(2,128)(2,1)S(1)} async-done(((bf16[4,2,3072]{2,1,0:T(2,128)(2,1)}), bf16[4,2,3072]{2,1,0:T(2,128)(2,1)S(1)}, u32[]{:S(2)}, u32[]{:S(2)}) %all-to-all-start) | async-done | bytes 49184 | tf_op jit(solution)/shard_map/all_to_all | solution.py:132
  186.8 4.6 %scatter_fusion.1 = f32[32,3,64]{2,1,0:T(4,128)S(1)} fusion(f32[32,3,64]{2,1,0:T(4,128)S(1)} %broadcast_in_dim.72, s32[128]{0:T(128)S(1)} %compare_select_fusion.2, f32[128,3,64]{2,1,0:T(4,128)S(1)} %copy.67), kind=kCustom, calls=%fused_computation.2 | custom fusion | bytes 295424 | tf_op jit(solution)/shard_map/scatter | solution.py:144
  192.1 90.7 %all-reduce.5.cloned.1.call-done = bf16[512,2048]{1,0:T(8,128)(2,1)} async-done(((bf16[512,2048]{1,0:T(8,128)(2,1)}), bf16[512,2048]{1,0:T(8,128)(2,1)}) %all-reduce.5.cloned.1.call-update) | async-done | bytes 2097168 | tf_op jit(solution)/shard_map/psum | solution.py:115
  282.8 2.5 fusion
  285.3 1.8 fusion.11
  287.1 4.0 %bitcast_convert_fusion = f32[128,64,128]{2,1,0:T(8,128)} fusion(bf16[128,1,64,128]{3,2,1,0:T(8,128)(2,1)} %all-gather.3.cloned.1.call-done), kind=kLoop, calls=%fused_computation.29 | loop fusion | flops 1048576 | bytes 6291456 | tf_op jit(solution)/shard_map/convert_element_type | solution.py:128
  291.2 12.8 %scatter_fusion = f32[32,64,128]{2,1,0:T(8,128)S(1)} fusion(f32[32,64,128]{2,1,0:T(8,128)S(1)} %broadcast_in_dim.70, s32[128]{0:T(128)S(1)} %compare_select_fusion.2, f32[128,64,128]{2,1,0:T(8,128)} %bitcast_convert_fusion), kind=kCustom, calls=%fused_computation.1 | custom fusion | bytes 12583424 | tf_op jit(solution)/shard_map/scatter | solution.py:143
  304.0 1.0 copy-done.1
  (169 shorter events, 17.8 us)
Async XLA Ops:
  8.0 277.3 %copy-start = (bf16[2048,3,64]{0,2,1:T(8,128)(2,1)S(1)}, bf16[2048,3,64]{0,2,1:T(8,128)(2,1)}, u32[]{:S(2)}) copy-start(bf16[2048,3,64]{0,2,1:T(8,128)(2,1)} %param.33) | copy-start | bytes 2359300
  8.0 157.2 %all-reduce.3.cloned.1.call-start = ((), (), s32[]{:S(2)}) async-start(), calls=%async_computation.1 | async-start | bytes 4194304 | tf_op jit(solution)/shard_map/psum | solution.py:104
  9.3 8.1 %copy-start.7 = (s32[32]{0:T(128)S(1)}, s32[32]{0:T(128)}, u32[]{:S(2)}) copy-start(s32[32]{0:T(128)} %param.24) | copy-start | bytes 388
  10.5 5.8 %collective-permute-start = (bf16[512,2,64]{2,0,1:T(8,128)(2,1)S(1)}, bf16[512,2,64]{2,0,1:T(8,128)(2,1)S(1)}, u32[]{:S(2)}, u32[]{:S(2)}) collective-permute-start(bf16[512,2,64]{2,0,1:T(8,128)(2,1)S(1)} %copy.72), channel_id=1, source_target_pairs={{0,4},{4,0},{8,12},{12,8},{16,20},{20,16},{24,28},{28,24},{32,36},... | collective-permute-start | bytes 393224 | tf_op jit(solution)/shard_map/ppermute | solution.py:16
  14.5 0.7 copy-start.4
  17.4 35.1 %copy-start.6 = (f32[64]{0:T(128)S(1)}, f32[64]{0:T(128)}, u32[]{:S(2)}) copy-start(f32[64]{0:T(128)} %param.26) | copy-start | bytes 772
  52.4 116.1 %copy-start.2 = (bf16[32,1,64,128]{3,2,1,0:T(8,128)(2,1)}, bf16[32,1,64,128]{3,2,1,0:T(8,128)(2,1)S(1)}, u32[]{:S(2)}) copy-start(bf16[32,1,64,128]{3,2,1,0:T(8,128)(2,1)S(1)} %get-tuple-element.159) | copy-start | bytes 1572868
  55.6 113.0 %copy-start.8 = (f32[2048]{0:T(1024)S(1)}, f32[2048]{0:T(1024)}, u32[]{:S(2)}) copy-start(f32[2048]{0:T(1024)} %param.28) | copy-start | bytes 24580
  55.6 227.2 %all-reduce.5.cloned.1.call-start = ((), (), s32[]{:S(2)}) async-start(), calls=%async_computation.2 | async-start | bytes 4194304 | tf_op jit(solution)/shard_map/psum | solution.py:115
  170.6 5.1 %copy-start.5 = (bf16[32,19,64]{2,0,1:T(8,128)(2,1)S(1)}, bf16[32,19,64]{2,0,1:T(8,128)(2,1)}, u32[]{:S(2)}) copy-start(bf16[32,19,64]{2,0,1:T(8,128)(2,1)} %copy-done.4) | copy-start | bytes 233476
  170.6 11.6 %copy-start.10 = (s32[128]{0:T(128)S(1)}, s32[128]{0:T(128)}, u32[]{:S(2)}) copy-start(s32[128]{0:T(128)} %param.25) | copy-start | bytes 1540
  174.8 110.4 %copy-start.9 = (f32[2048]{0:T(1024)S(1)}, f32[2048]{0:T(1024)}, u32[]{:S(2)}) copy-start(f32[2048]{0:T(1024)} %param.32) | copy-start | bytes 24580
  174.9 112.2 %all-gather.3.cloned.1.call-start = ((), (), s32[]{:S(2)}) async-start(), calls=%async_computation.3 | async-start | bytes 2621440 | tf_op jit(solution)/shard_map/all_gather | solution.py:128
  178.2 8.4 %all-to-all-start = ((bf16[4,2,3072]{2,1,0:T(2,128)(2,1)}), bf16[4,2,3072]{2,1,0:T(2,128)(2,1)S(1)}, u32[]{:S(2)}, u32[]{:S(2)}) async-start(bf16[4,2,3072]{2,1,0:T(2,128)(2,1)} %reshape.293), calls=%async_computation | async-start | bytes 98304 | tf_op jit(solution)/shard_map/all_to_all | solution.py:132
  282.8 2.5 copy-start.3
  304.0 1.0 copy-start.1
Sparse Core Ops, SparseCore 0:
  55.7 109.5 all-reduce.2
  175.0 107.7 all-reduce.4
Sparse Core Ops, SparseCore 1:
  177.6 30.0 all-gather.2
